TPU v7x, 256 devices: a whole 4x4x8 slice. The times are simulated.
256 devices in a mesh: expert: 32 (over y, x, core), tensor: 8 (over z).
Axes of the slice: x: 4, y: 4, z: 8, core: 2. Of those that a mesh axis runs over, the one named last changes fastest.
Arguments:
- tokens: bfloat16 [16384, 4096], P('expert', 'tensor'), may hold values from -36 to 36
- expert_ids: int32 [16384, 1], P('expert'), may hold values from 0 to 63; in each aligned block of 512 rows (0 to 511, 512 to 1023, ...) at most 16 rows name the same one
- gates: float32 [16384, 1], P('expert'), may hold values from 0.25 to 1
- expert_in: bfloat16 [64, 4096, 2048], P('expert', 'tensor'), may hold values from -0.09375 to 0.09375
- expert_out: bfloat16 [64, 2048, 4096], P('expert', None, 'tensor'), may hold values from -0.125 to 0.125
- norm_gain: float32 [4096], replicated, may hold values from 0.5 to 2
- up_weight: bfloat16 [4096, 8192], P('expert', 'tensor'), may hold values from -0.09375 to 0.09375
- down_weight: bfloat16 [4096, 8192], P('expert', 'tensor'), may hold values from -0.0625 to 0.0625
Outputs:
- layer_output: bfloat16 [16384, 4096], P('expert', 'tensor')
Inputs may be any that keep to these rules, and one draw needn't show every extreme that they name: `expert_ids`: among the 512 tokens of one block, at most 16 carry the same expert id; in some blocks one id is carried by exactly 16 tokens.
All inputs are finite; a program needn't handle non-finite values.
Results may differ from a plain program's by a relative error of at most 0.015.
Values may be sent and summed in bfloat16 or wider, within the bound.
No kernel may reach another device: no remote copies, remote signals or barrier semaphores. Data moves between devices by JAX's collectives and lax.ppermute only.
A program may use at most 128 MiB of HBM per device.

v0:
```python
import jax
import jax.numpy as jnp
from jax import lax
from jax.sharding import PartitionSpec as P

EXP_DEV = 2


def slot_table(expert_col, experts, capacity):
    expert = expert_col[:, 0]
    count = expert.shape[0]
    order = jnp.arange(count, dtype=jnp.int32)
    same = (expert[:, None] == expert[None, :]) & (order[None, :] < order[:, None])
    position = jnp.sum(same.astype(jnp.int32), axis=1)
    slot_index = expert * capacity + position
    selector = jnp.arange(experts * capacity, dtype=jnp.int32)[:, None] == slot_index[None, :]
    return selector.astype(jnp.bfloat16)


def trade(buffer):
    result = lax.all_to_all(buffer, "expert", split_axis=0, concat_axis=0, tiled=True)
    return result


def gather_rows(weight, combine, start_value):
    return combine(start_value, lax.all_gather(weight, "expert", axis=0, tiled=True), jnp.int32(0))


def shards(tokens, expert_ids, gates, expert_in, expert_out, norm_gain, up_weight, down_weight):
    token_count = tokens.shape[0]
    local_width = tokens.shape[1]
    groups = lax.axis_size("expert")
    experts = EXP_DEV * groups
    capacity = 2 * token_count // experts
    selector = slot_table(expert_ids, experts, capacity)
    outgoing = jnp.dot(selector, tokens, preferred_element_type=jnp.float32).astype(jnp.bfloat16)
    outgoing = outgoing.reshape(groups, EXP_DEV, capacity, local_width)
    arrived = trade(outgoing)
    partial_value = jnp.einsum(
        "sjcd,jdh->sjch", arrived, expert_in, preferred_element_type=jnp.float32
    )
    summed = lax.psum(partial_value.astype(jnp.bfloat16), "tensor").astype(jnp.float32)
    active = jax.nn.relu(summed).astype(jnp.bfloat16)
    produced = jnp.einsum(
        "sjch,jhd->sjcd", active, expert_out, preferred_element_type=jnp.float32
    ).astype(jnp.bfloat16)
    returned = trade(produced).reshape(experts * capacity, local_width)
    routed = lax.dot_general(
        selector, returned, (((0,), (0,)), ((), ())), preferred_element_type=jnp.float32
    )
    mixed = (tokens.astype(jnp.float32) + gates * routed).astype(jnp.bfloat16)
    whole = lax.all_gather(mixed, "tensor", axis=1, tiled=True)
    whole_f32 = whole.astype(jnp.float32)
    mean_square = jnp.mean(whole_f32 * whole_f32, axis=1, keepdims=True)
    normed = (whole_f32 * lax.rsqrt(mean_square + 1e-06) * norm_gain).astype(jnp.bfloat16)

    def add_up(carry, piece, start):
        return jnp.dot(normed, piece, preferred_element_type=jnp.float32)

    ffn_hidden = gather_rows(
        up_weight, add_up, jnp.zeros((token_count, up_weight.shape[1]), jnp.float32)
    )
    ffn_active = jax.nn.gelu(ffn_hidden, approximate=True).astype(jnp.bfloat16)

    def add_down(carry, piece, start):
        contribution = lax.dot_general(
            ffn_active, piece, (((1,), (1,)), ((), ())), preferred_element_type=jnp.float32
        )
        return contribution

    outputs = gather_rows(
        down_weight, add_down, jnp.zeros((token_count, whole.shape[1]), jnp.float32)
    )
    summed_out = lax.psum_scatter(
        outputs.astype(jnp.bfloat16), "tensor", scatter_dimension=1, tiled=True
    ).astype(jnp.float32)
    return (mixed.astype(jnp.float32) + summed_out).astype(jnp.bfloat16)


def solution(mesh):
    return jax.shard_map(
        shards,
        mesh=mesh,
        in_specs=(
            P("expert", "tensor"),
            P("expert", None),
            P("expert", None),
            P("expert", "tensor", None),
            P("expert", None, "tensor"),
            P(),
            P("expert", "tensor"),
            P("expert", "tensor"),
        ),
        out_specs=P("expert", "tensor"),
        check_vma=False,
    )
```

profile of v0, /device:TPU:1, one launch (start us, length us, event | category | flops | bytes accessed | tf_op | source)
XLA Modules:
  0.0 422.7 jit_solution(1282529528484603267)
XLA Ops:
  6.5 0.0 all-reduce.2.cloned.1.call-start
  6.5 0.0 copy-start.1
  6.5 1.1 convert_reduce_fusion
  7.6 0.9 multiply_add_fusion
  8.5 1.8 fusion.24
  10.3 25.6 %all_to_all.10 = bf16[32,2,16,512]{3,2,1,0:T(8,128)(2,1)S(1)} all-to-all(bf16[32,2,16,512]{3,2,1,0:T(8,128)(2,1)S(1)} %bitcast.30), channel_id=1, replica_groups=mesh['expert'=32,'tensor'=8] {'expert'}, dimensions={0} | all-to-all | bytes 2097152 | tf_op jit(solution)/shard_map/all_to_all | solution.py:21
  35.8 0.0 copy-done.1
  35.8 4.3 %convert_bitcast_fusion = bf16[32,2,16,2048]{3,2,0,1:T(8,128)(2,1)} fusion(bf16[2,512,2048]{2,1,0:T(8,128)(2,1)S(1)} %copy-done.1, bf16[32,2,16,512]{3,2,1,0:T(8,128)(2,1)S(1)} %all_to_all.10), kind=kOutput, calls=%fused_computation.15 | convolution fusion | flops 2149580800 | bytes 9437184 | tf_op jit(solution)/shard_map/sjcd,jdh->sjch/dot_general | solution.py:39
  40.2 0.0 all-reduce.2.cloned.1.call-update
  40.2 0.0 all-gather.4.cloned.1.call-start
  40.2 108.1 %all-reduce.2.cloned.1.call-done = bf16[32,2,16,2048]{3,2,0,1:T(8,128)(2,1)} async-done(((bf16[32,2,16,2048]{3,2,0,1:T(8,128)(2,1)}), bf16[32,2,16,2048]{3,2,0,1:T(8,128)(2,1)}) %all-reduce.2.cloned.1.call-update) | async-done | bytes 4194320 | tf_op jit(solution)/shard_map/psum | solution.py:42
  148.3 5.8 %fusion.30 = bf16[32,2,16,512]{3,2,0,1:T(8,128)(2,1)S(1)} fusion(bf16[2,2048,512]{2,1,0:T(8,128)(2,1)} %param.12, bf16[32,2,16,2048]{3,2,0,1:T(8,128)(2,1)} %all-reduce.2.cloned.1.call-done), kind=kOutput, calls=%fused_computation.30 | convolution fusion | flops 2154299392 | bytes 9437184 | tf_op jit(solution)/shard_map/sjch,jhd->sjcd/dot_general | solution.py:44
  154.1 0.0 copy-start.2
  154.1 0.0 copy-start.4
  154.1 0.1 copy.15
  154.2 24.6 %all_to_all.11 = bf16[32,2,16,512]{3,2,1,0:T(8,128)(2,1)S(1)} all-to-all(bf16[32,2,16,512]{3,2,1,0:T(8,128)(2,1)S(1)} %copy.15), channel_id=1, replica_groups=mesh['expert'=32,'tensor'=8] {'expert'}, dimensions={0} | all-to-all | bytes 2097152 | tf_op jit(solution)/shard_map/all_to_all | solution.py:21
  178.8 0.0 copy-done.2
  178.9 0.0 copy-done.4
  178.9 0.0 copy-start.3
  178.9 1.6 fusion.35
  180.4 0.0 all-gather.4.cloned.1.call-update
  180.5 0.0 all-gather.6.cloned.1.call-start
  180.5 0.7 all-gather.6.cloned.1.call-update
  181.2 0.0 all-gather.8.cloned.1.call-start
  181.2 0.5 all-gather.8.cloned.1.call-update
  181.8 0.2 reduce-scatter.2.cloned.1.call-start
  182.0 48.4 %all-gather.4.cloned.1.call-done = bf16[512,4096]{1,0:T(8,128)(2,1)} async-done(((bf16[512,512]{1,0:T(8,128)(2,1)}), bf16[512,4096]{1,0:T(8,128)(2,1)}) %all-gather.4.cloned.1.call-update) | async-done | bytes 4194320 | tf_op jit(solution)/shard_map/all_gather | solution.py:52
  230.4 3.1 fusion
  233.4 56.4 %all-gather.6.cloned.1.call-done = bf16[4096,1024]{1,0:T(8,128)(2,1)} async-done(((bf16[128,1024]{1,0:T(8,128)(2,1)}), bf16[4096,1024]{1,0:T(8,128)(2,1)}) %all-gather.6.cloned.1.call-update) | async-done | bytes 8388624 | tf_op jit(solution)/shard_map/all_gather | solution.py:26
  289.9 0.0 copy-done.3
  289.9 9.6 %fusion.21 = bf16[512,1024]{1,0:T(8,128)(2,1)S(1)} fusion(bf16[4096,1024]{1,0:T(8,128)(2,1)} %all-gather.6.cloned.1.call-done, bf16[512,4096]{1,0:T(8,128)(2,1)} %all-gather.4.cloned.1.call-done, f32[4096]{0:T(1024)S(1)} %copy-done.3, f32[512]{0:T(512)S(1)} %add_rsqrt_fusion), kind=kOutput, calls=%fused_computation.24 | convolution fusion | flops 4308074496 | bytes 13649920 | tf_op jit(solution)/shard_map/dot_general | solution.py:58
  299.5 50.4 %all-gather.8.cloned.1.call-done = bf16[4096,1024]{1,0:T(8,128)(2,1)} async-done(((bf16[128,1024]{1,0:T(8,128)(2,1)}), bf16[4096,1024]{1,0:T(8,128)(2,1)}) %all-gather.8.cloned.1.call-update) | async-done | bytes 8388624 | tf_op jit(solution)/shard_map/all_gather | solution.py:26
  349.9 9.6 %convolution_convert_fusion = bf16[512,4096]{1,0:T(8,128)(2,1)} fusion(bf16[512,1024]{1,0:T(8,128)(2,1)S(1)} %fusion.21, bf16[4096,1024]{1,0:T(8,128)(2,1)} %all-gather.8.cloned.1.call-done), kind=kOutput, calls=%fused_computation.6 | convolution fusion | flops 4297064448 | bytes 13631488 | tf_op jit(solution)/shard_map/dot_general | solution.py:66
  359.5 0.0 copy-start
  359.5 0.0 reduce-scatter.2.cloned.1.call-update
  359.5 54.7 %reduce-scatter.2.cloned.1.call-done = bf16[512,512]{1,0:T(8,128)(2,1)} async-done(((bf16[512,4096]{1,0:T(8,128)(2,1)}), bf16[512,512]{1,0:T(8,128)(2,1)}) %reduce-scatter.2.cloned.1.call-update) | async-done | bytes 524304 | tf_op jit(solution)/shard_map/reduce_scatter | solution.py:74
  414.2 0.0 copy-done
  414.2 2.0 add_convert_fusion
  (1 shorter events, 0.0 us)
Async XLA Ops:
  6.5 141.8 %all-reduce.2.cloned.1.call-start = ((), (), s32[]{:S(2)}) async-start(), calls=%async_computation.3 | async-start | bytes 8388608 | tf_op jit(solution)/shard_map/psum | solution.py:42
  6.5 29.3 %copy-start.1 = (bf16[2,512,2048]{2,1,0:T(8,128)(2,1)S(1)}, bf16[2,512,2048]{2,1,0:T(8,128)(2,1)}, u32[]{:S(2)}) copy-start(bf16[2,512,2048]{2,1,0:T(8,128)(2,1)} %param.11) | copy-start | bytes 12582916
  40.2 190.2 %all-gather.4.cloned.1.call-start = ((), (), s32[]{:S(2)}) async-start(), calls=%async_computation.4 | async-start | bytes 4718592 | tf_op jit(solution)/shard_map/all_gather | solution.py:52
  154.1 24.7 %copy-start.2 = (bf16[512,512]{1,0:T(8,128)(2,1)S(1)}, bf16[512,512]{1,0:T(8,128)(2,1)}, u32[]{:S(2)}) copy-start(bf16[512,512]{1,0:T(8,128)(2,1)} %param.8) | copy-start | bytes 1572868
  154.1 24.7 %copy-start.4 = (f32[512,1]{0,1:T(1,128)S(1)}, f32[512,1]{0,1:T(1,128)}, u32[]{:S(2)}) copy-start(f32[512,1]{0,1:T(1,128)} %param.10) | copy-start | bytes 6148
  178.9 111.0 %copy-start.3 = (f32[4096]{0:T(1024)S(1)}, f32[4096]{0:T(1024)}, u32[]{:S(2)}) copy-start(f32[4096]{0:T(1024)} %param.13) | copy-start | bytes 49156
  180.5 109.4 %all-gather.6.cloned.1.call-start = ((), (), s32[]{:S(2)}) async-start(), calls=%async_computation.5 | async-start | bytes 8650752 | tf_op jit(solution)/shard_map/all_gather | solution.py:26
  181.2 168.7 %all-gather.8.cloned.1.call-start = ((), (), s32[]{:S(2)}) async-start(), calls=%async_computation.6 | async-start | bytes 8650752 | tf_op jit(solution)/shard_map/all_gather | solution.py:26
  181.8 232.5 %reduce-scatter.2.cloned.1.call-start = ((), (), s32[]{:S(2)}) async-start(), calls=%async_computation.7 | async-start | bytes 4718592 | tf_op jit(solution)/shard_map/reduce_scatter | solution.py:74
  359.5 54.8 %copy-start = (bf16[512,512]{1,0:T(8,128)(2,1)S(1)}, bf16[512,512]{1,0:T(8,128)(2,1)}, u32[]{:S(2)}) copy-start(bf16[512,512]{1,0:T(8,128)(2,1)} %fusion.35) | copy-start | bytes 1572868
Sparse Core Ops, SparseCore 0:
  40.3 107.9 all-reduce.1
  180.6 49.7 all-gather.3
  232.9 56.9 all-gather.5
  292.3 57.5 all-gather.7
  359.6 54.5 reduce-scatter.1
where the time goes:
time: 423 us
  waiting for transfers between devices  319 us (75%)
  blocking collectives  50.2 us (12%)
  matrix products  32.6 us (8%)
  between operations  13.2 us (3%)
  other arithmetic  7.03 us (2%)
    psum x1, waiting for transfers between devices, shards(): lax.psum(partial_value.astype(jnp.bfloat16), 'tensor').astype(jnp.float32)  108 us
    all_gather x2, waiting for transfers between devices, gather_rows(): lax.all_gather(weight, 'expert', axis=0, tiled=True)  107 us
    reduce_scatter x1, waiting for transfers between devices, shards(): lax.psum_scatter(outputs.astype(jnp.bfloat16), 'tensor', scatter_dimensio...  54.7 us
    all_to_all x2, blocking collectives, trade(): lax.all_to_all(buffer, 'expert', split_axis=0, concat_axis=0, tiled=True)  50.2 us
    all_gather x1, waiting for transfers between devices, shards(): whole = lax.all_gather(mixed, 'tensor', axis=1, tiled=True)  48.4 us
    dot_general x1, matrix products, add_up(): return jnp.dot(normed, piece, preferred_element_type=jnp.float32)  9.58 us
    dot_general x1, matrix products, add_down(): lax.dot_general(ffn_active, piece, (((1,), (1,)), ((), ())), preferred_el...  9.57 us
  transfers between devices with their start and end apart: 5, of which 5 were waited for; matrix products, arithmetic and copies ran while one was open for 3% of the time, Pallas kernels for 0%

commit v1 on v0

--- a/solution.py
+++ b/solution.py
@@ -23,7 +23,13 @@
 
 
 def gather_rows(weight, combine, start_value):
-    return combine(start_value, lax.all_gather(weight, "expert", axis=0, tiled=True), jnp.int32(0))
+    return combine(
+        start_value,
+        jnp.concatenate(
+            lax.all_to_all(jnp.stack([weight] * lax.axis_size("expert")), "expert", 0, 0), axis=0
+        ),
+        jnp.int32(0),
+    )
 
 
 def shards(tokens, expert_ids, gates, expert_in, expert_out, norm_gain, up_weight, down_weight):

time: 423 us -> 477 us (1.13)
  waiting for transfers between devices: 319 us -> 349 us
  starting transfers between devices: 0.34 us -> 16.6 us
  local copies, waits for them, and re-layouts: 0.09 us -> 8.9 us
    all_to_all x0 -> x2, waiting for transfers between devices: none -> 186 us  [gather_rows(): lax.all_to_all(jnp.stack([weight] * lax.axis_size('expert')), 'expert', 0...]
    all_gather x2 -> x0, waiting for transfers between devices: 107 us -> none  [gather_rows(): lax.all_gather(weight, 'expert', axis=0, tiled=True)]
    all_gather x1, waiting for transfers between devices: 48.4 us -> 0.02 us  [shards(): whole = lax.all_gather(mixed, 'tensor', axis=1, tiled=True)]
    all_to_all x0 -> x2, starting transfers between devices: none -> 16.3 us  [gather_rows(): lax.all_to_all(jnp.stack([weight] * lax.axis_size('expert')), 'expert', 0...]
    another operation x0 -> x2, local copies, waits for them, and re-layouts: none -> 8.6 us  [gather_rows(): jnp.stack([weight] * lax.axis_size('expert'))]
  transfers between devices with their start and end apart: 5 -> 5, of which waited for: 5 -> 4; matrix products, arithmetic and copies ran while one was open for 3% -> 4% of each run, Pallas kernels for 0% -> 0%
where the time goes in v1:
time: 477 us
  waiting for transfers between devices  349 us (73%)
  blocking collectives  50.1 us (11%)
  matrix products  31.3 us (7%)
  starting transfers between devices  16.6 us (3%)
  between operations  13.2 us (3%)
  local copies, waits for them, and re-layouts  8.9 us (2%)
  other arithmetic  7.18 us (2%)
    all_to_all x2, waiting for transfers between devices, gather_rows(): lax.all_to_all(jnp.stack([weight] * lax.axis_size('expert')), 'expert', 0...  186 us
    psum x1, waiting for transfers between devices, shards(): lax.psum(partial_value.astype(jnp.bfloat16), 'tensor').astype(jnp.float32)  108 us
    reduce_scatter x1, waiting for transfers between devices, shards(): lax.psum_scatter(outputs.astype(jnp.bfloat16), 'tensor', scatter_dimensio...  55.5 us
    all_to_all x2, blocking collectives, trade(): lax.all_to_all(buffer, 'expert', split_axis=0, concat_axis=0, tiled=True)  50.1 us
    all_to_all x2, starting transfers between devices, gather_rows(): lax.all_to_all(jnp.stack([weight] * lax.axis_size('expert')), 'expert', 0...  16.3 us
  transfers between devices with their start and end apart: 5, of which 4 were waited for; matrix products, arithmetic and copies ran while one was open for 4% of the time, Pallas kernels for 0%

profile of v1, /device:TPU:1, one launch (start us, length us, event | category | flops | bytes accessed | tf_op | source)
XLA Modules:
  0.0 476.7 jit_solution(17144688661011771425)
XLA Ops:
  6.5 0.0 all-reduce.2.cloned.1.call-start
  6.5 0.0 copy-start.4
  6.5 1.1 convert_reduce_fusion
  7.6 0.9 multiply_add_fusion
  8.5 1.8 fusion.24
  10.3 25.6 %all_to_all.20 = bf16[32,2,16,512]{3,2,1,0:T(8,128)(2,1)S(1)} all-to-all(bf16[32,2,16,512]{3,2,1,0:T(8,128)(2,1)S(1)} %bitcast.32), channel_id=1, replica_groups=mesh['expert'=32,'tensor'=8] {'expert'}, dimensions={0} | all-to-all | bytes 2097152 | tf_op jit(solution)/shard_map/all_to_all | solution.py:21
  35.8 0.0 copy-done.4
  35.8 4.3 convert_bitcast_fusion
  40.2 0.0 all-reduce.2.cloned.1.call-update
  40.2 108.1 %all-reduce.2.cloned.1.call-done = bf16[32,2,16,2048]{3,2,0,1:T(8,128)(2,1)} async-done(((bf16[32,2,16,2048]{3,2,0,1:T(8,128)(2,1)}), bf16[32,2,16,2048]{3,2,0,1:T(8,128)(2,1)}) %all-reduce.2.cloned.1.call-update) | async-done | bytes 4194320 | tf_op jit(solution)/shard_map/psum | solution.py:48
  148.3 5.8 %fusion.30 = bf16[32,2,16,512]{3,2,0,1:T(8,128)(2,1)S(1)} fusion(bf16[2,2048,512]{2,1,0:T(8,128)(2,1)} %param.12, bf16[32,2,16,2048]{3,2,0,1:T(8,128)(2,1)} %all-reduce.2.cloned.1.call-done), kind=kOutput, calls=%fused_computation.30 | convolution fusion | flops 2154299392 | bytes 9437184 | tf_op jit(solution)/shard_map/sjch,jhd->sjcd/dot_general | solution.py:50
  154.1 0.0 copy-start.2
  154.1 0.1 copy.15
  154.2 24.5 %all_to_all.21 = bf16[32,2,16,512]{3,2,1,0:T(8,128)(2,1)S(1)} all-to-all(bf16[32,2,16,512]{3,2,1,0:T(8,128)(2,1)S(1)} %copy.15), channel_id=1, replica_groups=mesh['expert'=32,'tensor'=8] {'expert'}, dimensions={0} | all-to-all | bytes 2097152 | tf_op jit(solution)/shard_map/all_to_all | solution.py:21
  178.7 0.0 copy-done.2
  178.7 4.3 stack.4
  183.0 0.0 copy-start.5
  183.0 0.0 copy-start.7
  183.0 5.1 %all-to-all-start.2 = ((bf16[32,128,1024]{2,1,0:T(8,128)(2,1)}), bf16[32,128,1024]{2,1,0:T(8,128)(2,1)}, u32[]{:S(2)}, u32[]{:S(2)}) async-start(bf16[32,128,1024]{2,1,0:T(8,128)(2,1)} %stack.4), calls=%async_computation.2 | async-start | bytes 16777216 | tf_op jit(solution)/shard_map/all_to_all | solution.py:29
  188.1 0.0 copy-start.3
  188.1 0.0 all-gather.2.cloned.1.call-start
  188.1 0.0 copy-done.5
  188.2 0.0 copy-done.7
  188.2 1.6 fusion.35
  189.7 0.0 all-gather.2.cloned.1.call-update
  189.8 98.1 %all-to-all-done.2 = bf16[32,128,1024]{2,1,0:T(8,128)(2,1)} async-done(((bf16[32,128,1024]{2,1,0:T(8,128)(2,1)}), bf16[32,128,1024]{2,1,0:T(8,128)(2,1)}, u32[]{:S(2)}, u32[]{:S(2)}) %all-to-all-start.2) | async-done | bytes 8388640 | tf_op jit(solution)/shard_map/all_to_all | solution.py:29
  287.9 0.0 copy-done.3
  287.9 4.3 stack.5
  292.2 0.0 copy-start.6
  292.2 11.2 %all-to-all-start.3 = ((bf16[32,128,1024]{2,1,0:T(8,128)(2,1)}), bf16[32,128,1024]{2,1,0:T(8,128)(2,1)}, u32[]{:S(2)}, u32[]{:S(2)}) async-start(bf16[32,128,1024]{2,1,0:T(8,128)(2,1)} %stack.5), calls=%async_computation.3 | async-start | bytes 16777216 | tf_op jit(solution)/shard_map/all_to_all | solution.py:29
  303.4 0.2 reduce-scatter.2.cloned.1.call-start
  303.6 0.0 all-gather.2.cloned.1.call-done
  303.7 0.0 copy-start
  303.7 3.2 fusion
  306.9 0.0 copy-done.6
  306.9 0.2 copy-done
  307.1 8.4 %fusion.21 = bf16[512,1024]{1,0:T(8,128)(2,1)S(1)} fusion(bf16[4096,1024]{1,0:T(8,128)(2,1)} %bitcast.10, bf16[512,4096]{1,0:T(8,128)(2,1)S(1)} %copy-done, f32[4096]{0:T(1024)S(1)} %copy-done.6, f32[512]{0:T(512)S(1)} %add_rsqrt_fusion), kind=kOutput, calls=%fused_computation.24 | convolution fusion | flops 4308074496 | bytes 13649920 | tf_op jit(solution)/shard_map/dot_general | solution.py:64
  315.5 87.7 %all-to-all-done.3 = bf16[32,128,1024]{2,1,0:T(8,128)(2,1)} async-done(((bf16[32,128,1024]{2,1,0:T(8,128)(2,1)}), bf16[32,128,1024]{2,1,0:T(8,128)(2,1)}, u32[]{:S(2)}, u32[]{:S(2)}) %all-to-all-start.3) | async-done | bytes 8388640 | tf_op jit(solution)/shard_map/all_to_all | solution.py:29
  403.2 9.5 %convolution_convert_fusion = bf16[512,4096]{1,0:T(8,128)(2,1)} fusion(bf16[512,1024]{1,0:T(8,128)(2,1)S(1)} %fusion.21, bf16[4096,1024]{1,0:T(8,128)(2,1)} %bitcast.11), kind=kOutput, calls=%fused_computation.6 | convolution fusion | flops 4297064448 | bytes 13631488 | tf_op jit(solution)/shard_map/dot_general | solution.py:72
  412.6 0.0 copy-start.1
  412.6 0.0 reduce-scatter.2.cloned.1.call-update
  412.7 55.5 %reduce-scatter.2.cloned.1.call-done = bf16[512,512]{1,0:T(8,128)(2,1)} async-done(((bf16[512,4096]{1,0:T(8,128)(2,1)}), bf16[512,512]{1,0:T(8,128)(2,1)}) %reduce-scatter.2.cloned.1.call-update) | async-done | bytes 524304 | tf_op jit(solution)/shard_map/reduce_scatter | solution.py:80
  468.2 0.0 copy-done.1
  468.2 2.0 add_convert_fusion
  (1 shorter events, 0.0 us)
Async XLA Ops:
  6.5 141.8 %all-reduce.2.cloned.1.call-start = ((), (), s32[]{:S(2)}) async-start(), calls=%async_computation.5 | async-start | bytes 8388608 | tf_op jit(solution)/shard_map/psum | solution.py:48
  6.5 29.3 %copy-start.4 = (bf16[2,512,2048]{2,1,0:T(8,128)(2,1)S(1)}, bf16[2,512,2048]{2,1,0:T(8,128)(2,1)}, u32[]{:S(2)}) copy-start(bf16[2,512,2048]{2,1,0:T(8,128)(2,1)} %param.11) | copy-start | bytes 12582916
  154.1 24.6 %copy-start.2 = (bf16[128,1024]{1,0:T(8,128)(2,1)S(1)}, bf16[128,1024]{1,0:T(8,128)(2,1)}, u32[]{:S(2)}) copy-start(bf16[128,1024]{1,0:T(8,128)(2,1)} %param.14) | copy-start | bytes 786436
  183.0 5.1 %copy-start.5 = (bf16[512,512]{1,0:T(8,128)(2,1)S(1)}, bf16[512,512]{1,0:T(8,128)(2,1)}, u32[]{:S(2)}) copy-start(bf16[512,512]{1,0:T(8,128)(2,1)} %param.8) | copy-start | bytes 1572868
  183.0 5.2 %copy-start.7 = (f32[512,1]{0,1:T(1,128)S(1)}, f32[512,1]{0,1:T(1,128)}, u32[]{:S(2)}) copy-start(f32[512,1]{0,1:T(1,128)} %param.10) | copy-start | bytes 6148
  183.0 104.9 %all-to-all-start.2 = ((bf16[32,128,1024]{2,1,0:T(8,128)(2,1)}), bf16[32,128,1024]{2,1,0:T(8,128)(2,1)}, u32[]{:S(2)}, u32[]{:S(2)}) async-start(bf16[32,128,1024]{2,1,0:T(8,128)(2,1)} %stack.4), calls=%async_computation.2 | async-start | bytes 16777216 | tf_op jit(solution)/shard_map/all_to_all | solution.py:29
  188.1 99.8 %copy-start.3 = (bf16[128,1024]{1,0:T(8,128)(2,1)S(1)}, bf16[128,1024]{1,0:T(8,128)(2,1)}, u32[]{:S(2)}) copy-start(bf16[128,1024]{1,0:T(8,128)(2,1)} %param.15) | copy-start | bytes 786436
  188.1 115.6 %all-gather.2.cloned.1.call-start = ((), (), s32[]{:S(2)}) async-start(), calls=%async_computation.6 | async-start | bytes 4718592 | tf_op jit(solution)/shard_map/all_gather | solution.py:58
  292.2 14.7 %copy-start.6 = (f32[4096]{0:T(1024)S(1)}, f32[4096]{0:T(1024)}, u32[]{:S(2)}) copy-start(f32[4096]{0:T(1024)} %param.13) | copy-start | bytes 49156
  292.2 111.0 %all-to-all-start.3 = ((bf16[32,128,1024]{2,1,0:T(8,128)(2,1)}), bf16[32,128,1024]{2,1,0:T(8,128)(2,1)}, u32[]{:S(2)}, u32[]{:S(2)}) async-start(bf16[32,128,1024]{2,1,0:T(8,128)(2,1)} %stack.5), calls=%async_computation.3 | async-start | bytes 16777216 | tf_op jit(solution)/shard_map/all_to_all | solution.py:29
  303.4 164.8 %reduce-scatter.2.cloned.1.call-start = ((), (), s32[]{:S(2)}) async-start(), calls=%async_computation.7 | async-start | bytes 4718592 | tf_op jit(solution)/shard_map/reduce_scatter | solution.py:80
  303.7 3.5 copy-start
  412.6 55.5 %copy-start.1 = (bf16[512,512]{1,0:T(8,128)(2,1)S(1)}, bf16[512,512]{1,0:T(8,128)(2,1)}, u32[]{:S(2)}) copy-start(bf16[512,512]{1,0:T(8,128)(2,1)} %fusion.35) | copy-start | bytes 1572868
Sparse Core Ops, SparseCore 0:
  40.3 107.9 all-reduce.1
  190.7 53.4 all-gather.1
  412.8 55.3 reduce-scatter.1
